TPU v7x, 512 devices: a whole 4x4x16 slice. The times are simulated.
512 devices in a mesh: space: 32 (over z, core), tm: 16 (over x, y).
Axes of the slice: x: 4, y: 4, z: 16, core: 2. Of those that a mesh axis runs over, the one named last changes fastest.
Arguments:
- recordings: bfloat16 [2, 3, 512, 32768], P(None, None, 'space', 'tm'), may hold values from -30 to 30
- owner: int32 [512, 1], P('space'), may hold values from 0 to 31; in each aligned block of 16 rows (0 to 15, 16 to 31, ...) at most 2 rows name the same one
- valid_range: int32 [512, 2], P('space'), may hold values from 0 to 32768, as said below
- bin_mask: int32 [512, 96], P('space'), may hold values 0 or 1
Outputs:
- adjoint: bfloat16 [3, 2048, 32768], P(None, 'space', 'tm')
Inputs may be any that keep to these rules, and one draw needn't show every extreme that they name: `owner`: among the 16 receivers listed on one index of space, no subdomain owns more than 2; some subdomain owns exactly 2 of them. `valid_range`: column 0 is below column 1 in every row.
All inputs are finite; a program needn't handle non-finite values. No bound on the sum of `bin_mask` on one device may be relied on, other than what follows from the above.
Results may differ from a plain program's by a relative error of at most 0.013.
Values may be sent and summed in bfloat16 or wider, within the bound.
A program may use at most 128 MiB of HBM per device.

v0:
```python
import math
import jax
import jax.numpy as jnp
from jax import lax
from jax.sharding import PartitionSpec as P

BINS = 96
HOP = 256
HALO = 1024
KERNEL = 2304
WATER = 0.1
EPSILON = 1e-06


def with_halo(block, sides, width):
    for axis, dim in sides:
        count = lax.axis_size(axis)
        forward = [(i, i + 1) for i in range(count - 1)]
        backward = [(target, source) for source, target in forward]
        low = lax.ppermute(
            lax.slice_in_dim(block, block.shape[dim] - width, None, axis=dim), axis, forward
        )
        high = lax.ppermute(lax.slice_in_dim(block, 0, width, axis=dim), axis, backward)
        block = jnp.concatenate([low, block, high], axis=dim)
    return block


def shifted(block, axis, distance):
    devices = range(lax.axis_size(axis))
    route = [(i - distance, i) for i in devices if i - distance in devices]
    return lax.ppermute(block, axis, route)


def cq_kernel(kern_len, bins):
    octave_bins = bins // 8
    index = jnp.arange(bins).astype(jnp.float32)
    freq = 0.25 * jnp.exp2((index - (bins - 1)) / octave_bins)
    quality = 1.0 / (2.0 ** (1.0 / octave_bins) - 1.0)
    support = jnp.minimum(quality / freq, float(kern_len))
    offset = jnp.arange(kern_len).astype(jnp.float32) - 0.5 * (kern_len - 1)
    ratio = offset[:, None] / support[None, :]
    window = jnp.where(jnp.abs(ratio) < 0.5, 0.5 + 0.5 * jnp.cos(2.0 * math.pi * ratio), 0.0)
    window = window / jnp.sqrt(jnp.sum(window * window, axis=0, keepdims=True))
    cycles = offset[:, None] * freq[None, :]
    phase = cycles - jnp.floor(cycles)
    table = jnp.concatenate(
        [window * jnp.cos(2.0 * math.pi * phase), -window * jnp.sin(2.0 * math.pi * phase)], axis=1
    )
    return table.astype(jnp.bfloat16)


def adjoint_of(syn_re, syn_im, obs_re, obs_im, weight):
    level = (
        WATER * jnp.mean(obs_re * obs_re + obs_im * obs_im, axis=(-2, -1), keepdims=True) + EPSILON
    )
    syn_norm = jnp.sqrt(syn_re * syn_re + syn_im * syn_im + level)
    obs_norm = jnp.sqrt(obs_re * obs_re + obs_im * obs_im + level)
    diff_re = weight * (syn_re / syn_norm - obs_re / obs_norm)
    diff_im = weight * (syn_im / syn_norm - obs_im / obs_norm)
    inner = (syn_re * diff_re + syn_im * diff_im) / (syn_norm * syn_norm * syn_norm)
    return (diff_re / syn_norm - syn_re * inner, diff_im / syn_norm - syn_im * inner)


def analyse(blocks, table, frames):
    taps = table.shape[0] // HOP
    unfolded = jnp.concatenate([blocks[..., tap : tap + frames, :] for tap in range(taps)], axis=-1)
    return jnp.einsum("...fh,hk->...fk", unfolded, table, preferred_element_type=jnp.float32)


def synthesise(coefs, table, frames):
    taps = table.shape[0] // HOP
    term = jnp.einsum("...fk,hk->...fh", coefs, table, preferred_element_type=jnp.float32)
    term = term.reshape(term.shape[:-1] + (taps, HOP))
    lead = len(term.shape) - 3
    ext = jnp.zeros(coefs.shape[:-2] + (frames + taps - 1, HOP), jnp.float32)
    for tap in range(taps):
        widths = [(0, 0)] * lead + [(tap, taps - 1 - tap), (0, 0)]
        ext = ext + jnp.pad(term[..., tap, :], widths)
    return ext


def frame_weight(ranges, masks, frames_all):
    centers = jnp.arange(frames_all, dtype=jnp.int32) * HOP + HOP // 2
    inside = (ranges[:, 0:1] <= centers[None, :]) & (centers[None, :] < ranges[:, 1:2])
    return inside.astype(jnp.float32)[:, :, None] * masks.astype(jnp.float32)[:, None, :]


def misfit(coefs, weight):
    adj_re, adj_im = adjoint_of(
        coefs[0, ..., :BINS],
        coefs[0, ..., BINS:],
        coefs[1, ..., :BINS],
        coefs[1, ..., BINS:],
        weight,
    )
    joined = jnp.concatenate([adj_re, adj_im], axis=-1)
    return joined.reshape(joined.shape[:2] + (joined.shape[2] * joined.shape[3],)).astype(
        jnp.bfloat16
    )


def on_device(recordings, owner, valid_range, bin_mask):
    table = cq_kernel(KERNEL, BINS)
    margin = HALO // HOP
    width = 2 * BINS
    groups = lax.axis_size("tm")
    comps = recordings.shape[1]
    rec_dev = recordings.shape[2]
    samples_dev = recordings.shape[3]
    frames_dev = samples_dev // HOP
    rec_group = rec_dev // groups
    first_row = lax.axis_index("tm") * rec_group
    ranges = lax.dynamic_slice_in_dim(valid_range, first_row, rec_group, 0)
    masks = lax.dynamic_slice_in_dim(bin_mask, first_row, rec_group, 0)
    extended = with_halo(recordings, (("tm", 3),), HALO)
    blocks = extended.reshape(2, comps, rec_dev, frames_dev + 2 * margin, HOP)
    coefs = analyse(blocks, table, frames_dev)
    packed = coefs.astype(jnp.bfloat16).reshape(2, comps, rec_dev, frames_dev * width)
    weight = frame_weight(ranges, masks, frames_dev * groups)
    pieces = lax.all_to_all(packed, "tm", split_axis=2, concat_axis=3, tiled=True)
    items = pieces.shape[1]
    frames_all = pieces.shape[3] // width
    local_coefs = pieces.astype(jnp.float32).reshape(2, items, rec_group, frames_all, width)
    adjoint_local = misfit(local_coefs, weight)
    adjoint_back = lax.all_to_all(adjoint_local, "tm", split_axis=2, concat_axis=1, tiled=True)
    adjoint_frames = adjoint_back.reshape(comps, rec_dev, frames_dev, width)
    ext = synthesise(adjoint_frames, table, frames_dev)
    flat = ext.reshape(comps, rec_dev, (frames_dev + 2 * margin) * HOP)
    middle = flat[:, :, HALO : HALO + samples_dev]
    from_before = shifted(flat[:, :, HALO + samples_dev :].astype(jnp.bfloat16), "tm", 1).astype(
        jnp.float32
    )
    from_after = shifted(flat[:, :, :HALO].astype(jnp.bfloat16), "tm", -1).astype(jnp.float32)
    middle = middle.at[:, :, :HALO].add(from_before)
    middle = middle.at[:, :, samples_dev - HALO :].add(from_after)
    series = middle.astype(jnp.bfloat16)
    count = lax.axis_size("space")
    most = max(2, 3 * rec_dev // (2 * count))
    target = owner[:, 0]
    onehot = (target[:, None] == jnp.arange(count, dtype=jnp.int32)[None, :]).astype(jnp.int32)
    before = jnp.cumsum(onehot, axis=0) - onehot
    rank = jnp.sum(before * onehot, axis=1)
    slot = target * most + rank
    select = (jnp.arange(count * most, dtype=jnp.int32)[:, None] == slot[None, :]).astype(
        jnp.bfloat16
    )
    outgoing = jnp.einsum("sr,crt->cst", select, series, preferred_element_type=jnp.float32).astype(
        jnp.bfloat16
    )
    return lax.all_to_all(outgoing, "space", split_axis=1, concat_axis=1, tiled=True)


def solution(mesh):
    return jax.shard_map(
        on_device,
        mesh=mesh,
        in_specs=(
            P(None, None, "space", "tm"),
            P("space", None),
            P("space", None),
            P("space", None),
        ),
        out_specs=P(None, "space", "tm"),
        check_vma=False,
    )
```

profile of v0, /device:TPU:25, one launch (start us, length us, event | category | flops | bytes accessed | tf_op | source)
XLA Modules:
  0.0 347.0 jit_solution(11848009665123763137)
XLA Ops:
  0.0 1.1 fusion.24
  1.1 2.8 collective-permute-start
  3.9 2.5 collective-permute-start.1
  6.5 3.4 multiply_reduce_fusion
  9.9 6.7 %multiply_convert_fusion.3 = (bf16[2304,96]{0,1:T(8,128)(2,1)S(1)}, bf16[2304,96]{0,1:T(8,128)(2,1)S(1)}) fusion(f32[96]{0:T(128)S(1)} %get-tuple-element.51, f32[2304]{0:T(1024)S(1)} %convert_add_fusion.1, f32[96]{0:T(128)S(1)} %sqrt.38, f32[96]{0:T(128)S(1)} %get-tuple-element.50), kind=kLoop, calls=%fused_computation.19 | loop fusion | flops 3760128 | bytes 895104 | tf_op jit(solution)/shard_map/convert.7
  16.6 6.8 %multiply_convert_fusion.1 = (bf16[9,256,96]{1,2,0:T(8,128)(2,1)S(1)}, bf16[9,256,96]{1,2,0:T(8,128)(2,1)S(1)}) fusion(f32[96]{0:T(128)S(1)} %get-tuple-element.51, f32[9,256]{1,0:T(8,128)S(1)} %convert_add_fusion, f32[96]{0:T(128)S(1)} %sqrt.38, f32[96]{0:T(128)S(1)} %get-tuple-element.50), kind=kLoop, calls=%fused_computation.15 | loop fusion | flops 3760128 | bytes 895104 | tf_op jit(solution)/shard_map/convert.3
  23.5 0.7 fusion.19
  24.2 0.5 fusion.25
  25.9 1.1 convolution_convert_fusion.1
  27.4 1.0 copy.61
  28.4 6.6 %all-to-all-start = ((bf16[2,3,16,1536]{3,0,1,2:T(2,128)(2,1)}), bf16[2,3,16,1536]{3,0,1,2:T(2,128)(2,1)S(1)}, u32[]{:S(2)}, u32[]{:S(2)}) async-start(bf16[2,3,16,1536]{3,0,1,2:T(2,128)(2,1)} %copy.61), calls=%async_computation | async-start | bytes 589824 | tf_op jit(solution)/shard_map/all_to_all | solution.py:120
  35.0 1.2 and_convert_fusion
  36.3 4.4 %all-to-all-done = bf16[2,3,16,1536]{3,0,1,2:T(2,128)(2,1)S(1)} async-done(((bf16[2,3,16,1536]{3,0,1,2:T(2,128)(2,1)}), bf16[2,3,16,1536]{3,0,1,2:T(2,128)(2,1)S(1)}, u32[]{:S(2)}, u32[]{:S(2)}) %all-to-all-start) | async-done | bytes 294944 | tf_op jit(solution)/shard_map/all_to_all | solution.py:120
  41.2 0.4 subtract_convert_fusion.1
  42.0 19.4 %copy.66 = bf16[3,1,24576]{0,1,2:T(2,128)(2,1)} copy(bf16[3,1,24576]{2,0,1:T(4,128)(2,1)S(1)} %convert_element_type.135) | data formatting | bytes 294912 | tf_op jit(solution)/shard_map/convert_element_type | solution.py:97
  61.4 0.5 broadcast.341
  61.9 134.9 %reduce.5 = bf16[24576,3]{1,0:T(8,128)(2,1)} reduce(bf16[24576,1,3]{2,1,0:T(2,128)(2,1)} %bitcast.152, bf16[]{:T(256)} %broadcast.341), dimensions={1}, to_apply=%bitcast.148.reduce_sub_computation | reduce | bytes 294914
  196.9 10.0 %reshape.529 = bf16[16,2,2304]{2,1,0:T(2,128)(2,1)} reshape(bf16[24576,3]{1,0:T(8,128)(2,1)} %reduce.5) | data formatting | bytes 294912
  206.9 5.5 %all-to-all-start.1 = ((bf16[16,2,2304]{2,1,0:T(2,128)(2,1)}), bf16[16,2,2304]{2,1,0:T(2,128)(2,1)S(1)}, u32[]{:S(2)}, u32[]{:S(2)}) async-start(bf16[16,2,2304]{2,1,0:T(2,128)(2,1)} %reshape.529), calls=%async_computation.1 | async-start | bytes 294912 | tf_op jit(solution)/shard_map/all_to_all | solution.py:125
  212.7 4.8 %all-to-all-done.1 = bf16[16,2,2304]{2,1,0:T(2,128)(2,1)S(1)} async-done(((bf16[16,2,2304]{2,1,0:T(2,128)(2,1)}), bf16[16,2,2304]{2,1,0:T(2,128)(2,1)S(1)}, u32[]{:S(2)}, u32[]{:S(2)}) %all-to-all-start.1) | async-done | bytes 147488 | tf_op jit(solution)/shard_map/all_to_all | solution.py:125
  217.5 14.4 %reshape.530 = bf16[24576,1,3]{2,1,0:T(2,128)(2,1)} reshape(bf16[16,2,2304]{2,1,0:T(2,128)(2,1)S(1)} %all-to-all-done.1) | data formatting | bytes 294912
  231.9 23.3 %copy.67 = bf16[3,1,24576]{2,0,1:T(4,128)(2,1)S(1)} copy(bf16[3,1,24576]{0,1,2:T(2,128)(2,1)} %bitcast.151) | data formatting | bytes 294912 | tf_op jit(solution)/shard_map/all_to_all | solution.py:125
  255.4 0.6 fusion.5
  256.1 0.4 slice_bitcast_fusion.8
  256.5 0.5 pad_add_fusion
  257.3 3.5 %collective-permute-start.2 = (bf16[3,16,1024]{2,1,0:T(8,128)(2,1)S(1)}, bf16[3,16,1024]{2,1,0:T(8,128)(2,1)S(1)}, u32[]{:S(2)}, u32[]{:S(2)}) collective-permute-start(bf16[3,16,1024]{2,1,0:T(8,128)(2,1)S(1)} %get-tuple-element.41), channel_id=1, source_target_pairs={{0,1},{1,2},{2,3},{3,4},{4,5},{5,6},{6,7},{7,8},{8,9},{9,10},{10,1... | collective-permute-start | bytes 294920 | tf_op jit(solution)/shard_map/ppermute | solution.py:31
  260.9 1.9 collective-permute-start.3
  262.8 5.5 %collective-permute-done.3 = bf16[3,16,1024]{2,1,0:T(8,128)(2,1)S(1)} collective-permute-done((bf16[3,16,1024]{2,1,0:T(8,128)(2,1)S(1)}, bf16[3,16,1024]{2,1,0:T(8,128)(2,1)S(1)}, u32[]{:S(2)}, u32[]{:S(2)}) %collective-permute-start.3) | collective-permute-done | bytes 98336 | tf_op jit(solution)/shard_map/ppermute | solution.py:31
  268.4 0.5 fusion
  268.9 0.7 copy.76
  269.5 76.0 %all_to_all.23 = bf16[3,64,2048]{2,0,1:T(4,128)(2,1)S(1)} all-to-all(bf16[3,64,2048]{2,0,1:T(4,128)(2,1)S(1)} %copy.76), channel_id=1, replica_groups=mesh['space'=32,'tm'=16] {'space'}, dimensions={1} | all-to-all | bytes 1572864 | tf_op jit(solution)/shard_map/all_to_all | solution.py:150
  345.5 1.5 copy.77
  (44 shorter events, 3.3 us)
Async XLA Ops:
  0.0 23.4 %copy-start = (s32[16,2]{0,1:T(2,128)S(1)}, s32[16,2]{0,1:T(2,128)}, u32[]{:S(2)}) copy-start(s32[16,2]{0,1:T(2,128)} %param.10) | copy-start | bytes 388
  0.0 24.7 %copy-start.1 = (bf16[2,3,16,2048]{3,2,1,0:T(8,128)(2,1)S(1)}, bf16[2,3,16,2048]{3,2,1,0:T(8,128)(2,1)}, u32[]{:S(2)}) copy-start(bf16[2,3,16,2048]{3,2,1,0:T(8,128)(2,1)} %param.8) | copy-start | bytes 1179652
  1.1 23.6 %collective-permute-start = (bf16[2,3,16,1024]{3,2,1,0:T(8,128)(2,1)S(1)}, bf16[2,3,16,1024]{3,2,1,0:T(8,128)(2,1)S(1)}, u32[]{:S(2)}, u32[]{:S(2)}) collective-permute-start(bf16[2,3,16,1024]{3,2,1,0:T(8,128)(2,1)S(1)} %get-tuple-element.42), channel_id=1, source_target_pairs={{0,1},{1,2},{2,3},{3,4},{4,5},{5,6},{6,7},{7,8},{8,9},{9,10},{10,1... | collective-permute-start | bytes 589832 | tf_op jit(solution)/shard_map/ppermute | solution.py:20
  3.9 20.8 %collective-permute-start.1 = (bf16[2,3,16,1024]{3,2,1,0:T(8,128)(2,1)S(1)}, bf16[2,3,16,1024]{3,2,1,0:T(8,128)(2,1)S(1)}, u32[]{:S(2)}, u32[]{:S(2)}) collective-permute-start(bf16[2,3,16,1024]{3,2,1,0:T(8,128)(2,1)S(1)} %get-tuple-element.43), channel_id=1, source_target_pairs={{1,0},{2,1},{3,2},{4,3},{5,4},{6,5},{7,6},{8,7},{9,8},{10,9},{11,1... | collective-permute-start | bytes 589832 | tf_op jit(solution)/shard_map/ppermute | solution.py:23
  28.4 12.3 %all-to-all-start = ((bf16[2,3,16,1536]{3,0,1,2:T(2,128)(2,1)}), bf16[2,3,16,1536]{3,0,1,2:T(2,128)(2,1)S(1)}, u32[]{:S(2)}, u32[]{:S(2)}) async-start(bf16[2,3,16,1536]{3,0,1,2:T(2,128)(2,1)} %copy.61), calls=%async_computation | async-start | bytes 589824 | tf_op jit(solution)/shard_map/all_to_all | solution.py:120
  196.9 15.5 %copy-start.2 = (s32[16,1]{0,1:T(1,128)S(1)}, s32[16,1]{0,1:T(1,128)}, u32[]{:S(2)}) copy-start(s32[16,1]{0,1:T(1,128)} %param.9) | copy-start | bytes 196
  206.9 10.6 %all-to-all-start.1 = ((bf16[16,2,2304]{2,1,0:T(2,128)(2,1)}), bf16[16,2,2304]{2,1,0:T(2,128)(2,1)S(1)}, u32[]{:S(2)}, u32[]{:S(2)}) async-start(bf16[16,2,2304]{2,1,0:T(2,128)(2,1)} %reshape.529), calls=%async_computation.1 | async-start | bytes 294912 | tf_op jit(solution)/shard_map/all_to_all | solution.py:125
  257.3 5.5 %collective-permute-start.2 = (bf16[3,16,1024]{2,1,0:T(8,128)(2,1)S(1)}, bf16[3,16,1024]{2,1,0:T(8,128)(2,1)S(1)}, u32[]{:S(2)}, u32[]{:S(2)}) collective-permute-start(bf16[3,16,1024]{2,1,0:T(8,128)(2,1)S(1)} %get-tuple-element.41), channel_id=1, source_target_pairs={{0,1},{1,2},{2,3},{3,4},{4,5},{5,6},{6,7},{7,8},{8,9},{9,10},{10,1... | collective-permute-start | bytes 294920 | tf_op jit(solution)/shard_map/ppermute | solution.py:31
  260.9 7.5 %collective-permute-start.3 = (bf16[3,16,1024]{2,1,0:T(8,128)(2,1)S(1)}, bf16[3,16,1024]{2,1,0:T(8,128)(2,1)S(1)}, u32[]{:S(2)}, u32[]{:S(2)}) collective-permute-start(bf16[3,16,1024]{2,1,0:T(8,128)(2,1)S(1)} %get-tuple-element.40), channel_id=1, source_target_pairs={{1,0},{2,1},{3,2},{4,3},{5,4},{6,5},{7,6},{8,7},{9,8},{10,9},{11,1... | collective-permute-start | bytes 294920 | tf_op jit(solution)/shard_map/ppermute | solution.py:31
where the time goes:
time: 348 us; the launch traced here: 347 us
  other arithmetic  156 us (45%)
  blocking collectives  76 us (22%)
  local copies, waits for them, and re-layouts  75.2 us (22%)
  starting transfers between devices  22.8 us (7%)
  waiting for transfers between devices  14.8 us (4%)
    unnamed x1, other arithmetic  135 us
    all_to_all x1, blocking collectives, on_device(): lax.all_to_all(outgoing, 'space', split_axis=1, concat_axis=1, tiled=True)  76 us
    unnamed x18, local copies, waits for them, and re-layouts  26 us
    all_to_all x1, local copies, waits for them, and re-layouts, on_device(): lax.all_to_all(adjoint_local, 'tm', split_axis=2, concat_axis=1, tiled=True)  23.3 us
    convert_element_type x2, local copies, waits for them, and re-layouts, misfit(): joined.reshape(joined.shape[:2] + (joined.shape[2] * joined.shape[3],))  19.7 us
    another operation x4, other arithmetic  13.9 us
  transfers between devices with their start and end apart: 6, of which 3 were waited for; matrix products, arithmetic and copies ran while one was open for 6% of the time, Pallas kernels for 0%

commit v1 on v0

--- a/solution.py
+++ b/solution.py
@@ -122,7 +122,12 @@
     frames_all = pieces.shape[3] // width
     local_coefs = pieces.astype(jnp.float32).reshape(2, items, rec_group, frames_all, width)
     adjoint_local = misfit(local_coefs, weight)
-    adjoint_back = lax.all_to_all(adjoint_local, "tm", split_axis=2, concat_axis=1, tiled=True)
+    adjoint_back = jnp.concatenate(
+        lax.all_to_all(
+            jnp.stack(jnp.split(adjoint_local, lax.axis_size("tm"), axis=2)), "tm", 0, 0
+        ),
+        axis=1,
+    )
     adjoint_frames = adjoint_back.reshape(comps, rec_dev, frames_dev, width)
     ext = synthesise(adjoint_frames, table, frames_dev)
     flat = ext.reshape(comps, rec_dev, (frames_dev + 2 * margin) * HOP)

time: 348 us -> 155 us (0.45)
  other arithmetic: 156 us -> 20.8 us
  local copies, waits for them, and re-layouts: 75.2 us -> 17.3 us
    unnamed x1 -> x0, other arithmetic: 135 us -> none
    all_to_all x1 -> x0, local copies, waits for them, and re-layouts: 23.3 us -> none  [on_device(): lax.all_to_all(adjoint_local, 'tm', split_axis=2, concat_axis=1, tiled=True)]
    convert_element_type x2 -> x1, local copies, waits for them, and re-layouts: 19.7 us -> 0.25 us  [misfit(): joined.reshape(joined.shape[:2] + (joined.shape[2] * joined.shape[3],))]
    unnamed x18 -> x30, local copies, waits for them, and re-layouts: 26 us -> 10.1 us
  transfers between devices with their start and end apart: 6 -> 6, of which waited for: 3 -> 3; matrix products, arithmetic and copies ran while one was open for 6% -> 13% of each run, Pallas kernels for 0% -> 0%
where the time goes in v1:
time: 155 us; the launch traced here: 154 us
  blocking collectives  76 us (49%)
  starting transfers between devices  22.8 us (15%)
  other arithmetic  20.8 us (13%)
  local copies, waits for them, and re-layouts  17.3 us (11%)
  waiting for transfers between devices  14.8 us (10%)
  matrix products  2.21 us (1%)
    all_to_all x1, blocking collectives, on_device(): lax.all_to_all(outgoing, 'space', split_axis=1, concat_axis=1, tiled=True)  76 us
    another operation x4, other arithmetic  13.9 us
    unnamed x30, local copies, waits for them, and re-layouts  10.1 us
    all_to_all x1, starting transfers between devices, on_device(): lax.all_to_all(packed, 'tm', split_axis=2, concat_axis=3, tiled=True)  6.61 us
    ppermute x2, waiting for transfers between devices, shifted(): return lax.ppermute(block, axis, route)  5.51 us
    all_to_all x1, starting transfers between devices, on_device(): lax.all_to_all(jnp.stack(jnp.split(adjoint_local, lax.axis_size('tm'), ax...  5.5 us
    ppermute x2, starting transfers between devices, shifted(): return lax.ppermute(block, axis, route)  5.46 us
    all_to_all x1, waiting for transfers between devices, on_device(): lax.all_to_all(jnp.stack(jnp.split(adjoint_local, lax.axis_size('tm'), ax...  4.97 us
  transfers between devices with their start and end apart: 6, of which 3 were waited for; matrix products, arithmetic and copies ran while one was open for 13% of the time, Pallas kernels for 0%

profile of v1, /device:TPU:25, one launch (start us, length us, event | category | flops | bytes accessed | tf_op | source)
XLA Modules:
  0.0 154.3 jit_solution(5021923016003726282)
XLA Ops:
  0.0 1.1 fusion.24
  1.1 2.8 %collective-permute-start = (bf16[2,3,16,1024]{3,2,1,0:T(8,128)(2,1)S(1)}, bf16[2,3,16,1024]{3,2,1,0:T(8,128)(2,1)S(1)}, u32[]{:S(2)}, u32[]{:S(2)}) collective-permute-start(bf16[2,3,16,1024]{3,2,1,0:T(8,128)(2,1)S(1)} %get-tuple-element.42), channel_id=1, source_target_pairs={{0,1},{1,2},{2,3},{3,4},{4,5},{5,6},{6,7},{7,8},{8,9},{9,10},{10,1... | collective-permute-start | bytes 589832 | tf_op jit(solution)/shard_map/ppermute | solution.py:20
  3.9 2.5 %collective-permute-start.1 = (bf16[2,3,16,1024]{3,2,1,0:T(8,128)(2,1)S(1)}, bf16[2,3,16,1024]{3,2,1,0:T(8,128)(2,1)S(1)}, u32[]{:S(2)}, u32[]{:S(2)}) collective-permute-start(bf16[2,3,16,1024]{3,2,1,0:T(8,128)(2,1)S(1)} %get-tuple-element.43), channel_id=1, source_target_pairs={{1,0},{2,1},{3,2},{4,3},{5,4},{6,5},{7,6},{8,7},{9,8},{10,9},{11,1... | collective-permute-start | bytes 589832 | tf_op jit(solution)/shard_map/ppermute | solution.py:23
  6.5 3.4 %multiply_reduce_fusion = f32[96]{0:T(128)S(1)} fusion(f32[96]{0:T(128)S(1)} %get-tuple-element.50, f32[2304]{0:T(1024)S(1)} %convert_add_fusion.1), kind=kLoop, calls=%fused_computation.20 | loop fusion | flops 1990560 | bytes 9984 | tf_op jit(solution)/shard_map/reduce_sum | solution.py:43
  9.9 6.7 %multiply_convert_fusion.3 = (bf16[2304,96]{0,1:T(8,128)(2,1)S(1)}, bf16[2304,96]{0,1:T(8,128)(2,1)S(1)}) fusion(f32[96]{0:T(128)S(1)} %get-tuple-element.51, f32[2304]{0:T(1024)S(1)} %convert_add_fusion.1, f32[96]{0:T(128)S(1)} %sqrt.38, f32[96]{0:T(128)S(1)} %get-tuple-element.50), kind=kLoop, calls=%fused_computation.19 | loop fusion | flops 3760128 | bytes 895104 | tf_op jit(solution)/shard_map/convert.7
  16.6 6.8 %multiply_convert_fusion.1 = (bf16[9,256,96]{1,2,0:T(8,128)(2,1)S(1)}, bf16[9,256,96]{1,2,0:T(8,128)(2,1)S(1)}) fusion(f32[96]{0:T(128)S(1)} %get-tuple-element.51, f32[9,256]{1,0:T(8,128)S(1)} %convert_add_fusion, f32[96]{0:T(128)S(1)} %sqrt.38, f32[96]{0:T(128)S(1)} %get-tuple-element.50), kind=kLoop, calls=%fused_computation.15 | loop fusion | flops 3760128 | bytes 895104 | tf_op jit(solution)/shard_map/convert.3
  23.5 0.7 fusion.19
  26.0 1.1 convolution_convert_fusion.1
  27.4 1.0 copy.75
  28.5 6.6 %all-to-all-start = ((bf16[2,3,16,1536]{3,0,1,2:T(2,128)(2,1)}), bf16[2,3,16,1536]{3,0,1,2:T(2,128)(2,1)S(1)}, u32[]{:S(2)}, u32[]{:S(2)}) async-start(bf16[2,3,16,1536]{3,0,1,2:T(2,128)(2,1)} %copy.75), calls=%async_computation | async-start | bytes 589824 | tf_op jit(solution)/shard_map/all_to_all | solution.py:120
  35.1 1.2 and_convert_fusion
  36.4 4.4 %all-to-all-done = bf16[2,3,16,1536]{3,0,1,2:T(2,128)(2,1)S(1)} async-done(((bf16[2,3,16,1536]{3,0,1,2:T(2,128)(2,1)}), bf16[2,3,16,1536]{3,0,1,2:T(2,128)(2,1)S(1)}, u32[]{:S(2)}, u32[]{:S(2)}) %all-to-all-start) | async-done | bytes 294944 | tf_op jit(solution)/shard_map/all_to_all | solution.py:120
  42.1 0.6 constant_dynamic-update-slice_fusion.15
  42.7 0.6 constant_dynamic-update-slice_fusion.14
  43.3 0.6 constant_dynamic-update-slice_fusion.13
  43.9 0.6 constant_dynamic-update-slice_fusion.12
  45.1 0.6 constant_dynamic-update-slice_fusion.10
  45.7 0.6 constant_dynamic-update-slice_fusion.9
  46.3 0.6 constant_dynamic-update-slice_fusion.8
  46.9 0.6 constant_dynamic-update-slice_fusion.7
  47.5 0.6 constant_dynamic-update-slice_fusion.6
  48.7 0.6 constant_dynamic-update-slice_fusion.4
  49.3 0.6 constant_dynamic-update-slice_fusion.3
  51.8 5.5 %all-to-all-start.1 = ((bf16[16,3,1,1536]{3,1,2,0:T(4,128)(2,1)}), bf16[16,3,1,1536]{3,1,2,0:T(4,128)(2,1)S(1)}, u32[]{:S(2)}, u32[]{:S(2)}) async-start(bf16[16,3,1,1536]{3,1,2,0:T(4,128)(2,1)} %constant_dynamic-update-slice_fusion), calls=%async_computation.1 | async-start | bytes 393216 | tf_op jit(solution)/shard_map/all_to_all | solution.py:126
  57.5 5.0 %all-to-all-done.1 = bf16[16,3,1,1536]{3,1,2,0:T(4,128)(2,1)S(1)} async-done(((bf16[16,3,1,1536]{3,1,2,0:T(4,128)(2,1)}), bf16[16,3,1,1536]{3,1,2,0:T(4,128)(2,1)S(1)}, u32[]{:S(2)}, u32[]{:S(2)}) %all-to-all-start.1) | async-done | bytes 147488 | tf_op jit(solution)/shard_map/all_to_all | solution.py:126
  62.7 0.6 fusion.5
  64.6 3.5 %collective-permute-start.2 = (bf16[3,16,1024]{2,1,0:T(8,128)(2,1)S(1)}, bf16[3,16,1024]{2,1,0:T(8,128)(2,1)S(1)}, u32[]{:S(2)}, u32[]{:S(2)}) collective-permute-start(bf16[3,16,1024]{2,1,0:T(8,128)(2,1)S(1)} %get-tuple-element.41), channel_id=1, source_target_pairs={{0,1},{1,2},{2,3},{3,4},{4,5},{5,6},{6,7},{7,8},{8,9},{9,10},{10,1... | collective-permute-start | bytes 294920 | tf_op jit(solution)/shard_map/ppermute | solution.py:31
  68.2 1.9 %collective-permute-start.3 = (bf16[3,16,1024]{2,1,0:T(8,128)(2,1)S(1)}, bf16[3,16,1024]{2,1,0:T(8,128)(2,1)S(1)}, u32[]{:S(2)}, u32[]{:S(2)}) collective-permute-start(bf16[3,16,1024]{2,1,0:T(8,128)(2,1)S(1)} %get-tuple-element.40), channel_id=1, source_target_pairs={{1,0},{2,1},{3,2},{4,3},{5,4},{6,5},{7,6},{8,7},{9,8},{10,9},{11,1... | collective-permute-start | bytes 294920 | tf_op jit(solution)/shard_map/ppermute | solution.py:31
  70.2 5.5 %collective-permute-done.3 = bf16[3,16,1024]{2,1,0:T(8,128)(2,1)S(1)} collective-permute-done((bf16[3,16,1024]{2,1,0:T(8,128)(2,1)S(1)}, bf16[3,16,1024]{2,1,0:T(8,128)(2,1)S(1)}, u32[]{:S(2)}, u32[]{:S(2)}) %collective-permute-start.3) | collective-permute-done | bytes 98336 | tf_op jit(solution)/shard_map/ppermute | solution.py:31
  76.2 0.7 copy.89
  76.9 76.0 %all_to_all.19 = bf16[3,64,2048]{2,0,1:T(4,128)(2,1)S(1)} all-to-all(bf16[3,64,2048]{2,0,1:T(4,128)(2,1)S(1)} %copy.89), channel_id=1, replica_groups=mesh['space'=32,'tm'=16] {'space'}, dimensions={1} | all-to-all | bytes 1572864 | tf_op jit(solution)/shard_map/all_to_all | solution.py:155
  152.9 1.5 copy.90
  (55 shorter events, 8.8 us)
Async XLA Ops:
  0.0 23.4 %copy-start = (s32[16,2]{0,1:T(2,128)S(1)}, s32[16,2]{0,1:T(2,128)}, u32[]{:S(2)}) copy-start(s32[16,2]{0,1:T(2,128)} %param.10) | copy-start | bytes 388
  0.0 24.8 %copy-start.1 = (bf16[2,3,16,2048]{3,2,1,0:T(8,128)(2,1)S(1)}, bf16[2,3,16,2048]{3,2,1,0:T(8,128)(2,1)}, u32[]{:S(2)}) copy-start(bf16[2,3,16,2048]{3,2,1,0:T(8,128)(2,1)} %param.8) | copy-start | bytes 1179652
  1.1 23.7 %collective-permute-start = (bf16[2,3,16,1024]{3,2,1,0:T(8,128)(2,1)S(1)}, bf16[2,3,16,1024]{3,2,1,0:T(8,128)(2,1)S(1)}, u32[]{:S(2)}, u32[]{:S(2)}) collective-permute-start(bf16[2,3,16,1024]{3,2,1,0:T(8,128)(2,1)S(1)} %get-tuple-element.42), channel_id=1, source_target_pairs={{0,1},{1,2},{2,3},{3,4},{4,5},{5,6},{6,7},{7,8},{8,9},{9,10},{10,1... | collective-permute-start | bytes 589832 | tf_op jit(solution)/shard_map/ppermute | solution.py:20
  3.9 20.9 %collective-permute-start.1 = (bf16[2,3,16,1024]{3,2,1,0:T(8,128)(2,1)S(1)}, bf16[2,3,16,1024]{3,2,1,0:T(8,128)(2,1)S(1)}, u32[]{:S(2)}, u32[]{:S(2)}) collective-permute-start(bf16[2,3,16,1024]{3,2,1,0:T(8,128)(2,1)S(1)} %get-tuple-element.43), channel_id=1, source_target_pairs={{1,0},{2,1},{3,2},{4,3},{5,4},{6,5},{7,6},{8,7},{9,8},{10,9},{11,1... | collective-permute-start | bytes 589832 | tf_op jit(solution)/shard_map/ppermute | solution.py:23
  27.1 30.1 %copy-start.2 = (s32[16,1]{0,1:T(1,128)S(1)}, s32[16,1]{0,1:T(1,128)}, u32[]{:S(2)}) copy-start(s32[16,1]{0,1:T(1,128)} %param.9) | copy-start | bytes 196
  28.5 12.3 %all-to-all-start = ((bf16[2,3,16,1536]{3,0,1,2:T(2,128)(2,1)}), bf16[2,3,16,1536]{3,0,1,2:T(2,128)(2,1)S(1)}, u32[]{:S(2)}, u32[]{:S(2)}) async-start(bf16[2,3,16,1536]{3,0,1,2:T(2,128)(2,1)} %copy.75), calls=%async_computation | async-start | bytes 589824 | tf_op jit(solution)/shard_map/all_to_all | solution.py:120
  51.8 10.8 %all-to-all-start.1 = ((bf16[16,3,1,1536]{3,1,2,0:T(4,128)(2,1)}), bf16[16,3,1,1536]{3,1,2,0:T(4,128)(2,1)S(1)}, u32[]{:S(2)}, u32[]{:S(2)}) async-start(bf16[16,3,1,1536]{3,1,2,0:T(4,128)(2,1)} %constant_dynamic-update-slice_fusion), calls=%async_computation.1 | async-start | bytes 393216 | tf_op jit(solution)/shard_map/all_to_all | solution.py:126
  64.6 5.5 %collective-permute-start.2 = (bf16[3,16,1024]{2,1,0:T(8,128)(2,1)S(1)}, bf16[3,16,1024]{2,1,0:T(8,128)(2,1)S(1)}, u32[]{:S(2)}, u32[]{:S(2)}) collective-permute-start(bf16[3,16,1024]{2,1,0:T(8,128)(2,1)S(1)} %get-tuple-element.41), channel_id=1, source_target_pairs={{0,1},{1,2},{2,3},{3,4},{4,5},{5,6},{6,7},{7,8},{8,9},{9,10},{10,1... | collective-permute-start | bytes 294920 | tf_op jit(solution)/shard_map/ppermute | solution.py:31
  68.2 7.5 %collective-permute-start.3 = (bf16[3,16,1024]{2,1,0:T(8,128)(2,1)S(1)}, bf16[3,16,1024]{2,1,0:T(8,128)(2,1)S(1)}, u32[]{:S(2)}, u32[]{:S(2)}) collective-permute-start(bf16[3,16,1024]{2,1,0:T(8,128)(2,1)S(1)} %get-tuple-element.40), channel_id=1, source_target_pairs={{1,0},{2,1},{3,2},{4,3},{5,4},{6,5},{7,6},{8,7},{9,8},{10,9},{11,1... | collective-permute-start | bytes 294920 | tf_op jit(solution)/shard_map/ppermute | solution.py:31
